TPU v7x, 128 devices: a whole 4x4x4 slice. The times are simulated.
128 devices in a mesh: ctx: 16 (over x, y), ch: 8 (over z, core).
Axes of the slice: x: 4, y: 4, z: 4, core: 2. Of those that a mesh axis runs over, the one named last changes fastest.
Arguments:
- pre_gate: bfloat16 [128, 131072], P('ch', 'ctx'), may hold values from -6 to 6
- value: bfloat16 [128, 131072], P('ch', 'ctx'), may hold values from -6 to 6
- post_gate: bfloat16 [128, 131072], P('ch', 'ctx'), may hold values from -6 to 6
- filter_taps: float32 [8, 131072], P('ch', 'ctx'), may hold values from -0.011048543 to 0.011048543, as said below
- skip: float32 [128], P('ch'), may hold values from -6 to 6
Outputs:
- mixed: bfloat16 [128, 131072], P(None, ('ctx', 'ch'))
Inputs may be any that keep to these rules, and one draw needn't show every extreme that they name: `filter_taps`: one row of taps for each filter group.
All inputs are finite; a program needn't handle non-finite values.
Results may differ from a plain program's by a relative error of at most 0.013.
Values may be sent and summed in bfloat16 or wider, within the bound.
A program may use at most 128 MiB of HBM per device.

v0:
```python
import jax
import jax.numpy as jnp
import numpy as np
import ml_dtypes
from jax import lax
from jax.experimental import pallas as pl
from jax.experimental.pallas import tpu as pltpu
from jax.sharding import PartitionSpec as P

MESH = pl.DeviceIdType.MESH
F32 = jnp.float32
BF16 = jnp.bfloat16

CTX_X, CTX_Y = 4, 4
CTX = 16
CH = 8
CHANNELS = 16
BLOCK = 8192
R = 256
Q = 512
PIECE = 1024


def build_tables():
    rows = np.arange(R)
    cols = np.arange(Q)
    first = 2 * np.pi * ((np.outer(2 * rows + 1, rows)) % 1024) / 1024.0
    forward = np.concatenate([np.cos(first), -np.sin(first)], axis=0)
    backward = np.concatenate([np.cos(first).T, np.sin(first).T], axis=1) * (2.0**-17)
    turn = 2 * np.pi * np.outer(2 * rows + 1, cols) / 2.0**19
    twiddle = np.stack([np.cos(turn), -np.sin(turn)])
    second = 2 * np.pi * (np.outer(cols, cols) % Q) / Q
    wr, wi = np.cos(second), -np.sin(second)
    table = np.concatenate([np.concatenate([wr, wi], 1), np.concatenate([-wi, wr], 1)], 0)
    half = lambda a: a.astype(np.float32).astype(ml_dtypes.bfloat16)
    return half(forward), half(backward), half(table), twiddle.astype(np.float32)


def kernel(
    pre, val, post, taps, skip, fwd_t, bwd_t, tab_t, tw_t, out,
    pre_v, val_v, taps_v, fwd_v, bwd_v, tab_v, tw_v,
    sig32, tap32, sig_send, tap_send, sig_recv, tap_recv, post_recv,
    spec_b, spec_z, spec_h, back_v, y32, lin32, y_send, y_recv, got32, out_v,
    load_sems, table_sems, sig_sems, tap_sems, post_sems, y_sems, out_sem,
):
    p = lax.axis_index("ctx")
    g = lax.axis_index("ch")

    loads = [
        pltpu.make_async_copy(a, b, load_sems.at[i])
        for i, (a, b) in enumerate([(taps, taps_v), (pre, pre_v), (val, val_v)])
    ]
    for c in loads:
        c.start()

    barrier = pltpu.get_barrier_semaphore()
    px, py = p // CTX_Y, p % CTX_Y
    peers = []
    for dx in (2, 1, 3, 0):
        for dy in (2, 1, 3, 0):
            if dx or dy:
                peers.append(((px + dx) % CTX_X) * CTX_Y + (py + dy) % CTX_Y)
    ch_peers = [(g + j) % CH for j in range(1, CH)]
    for o in peers:
        pl.semaphore_signal(barrier, inc=1, device_id=(o, g), device_id_type=MESH)
    for o in ch_peers:
        pl.semaphore_signal(barrier, inc=1, device_id=(p, o), device_id_type=MESH)

    tables = [
        pltpu.make_async_copy(a, b, table_sems.at[i])
        for i, (a, b) in enumerate(
            [(fwd_t, fwd_v), (tw_t, tw_v), (tab_t, tab_v), (bwd_t, bwd_v)]
        )
    ]
    for c in tables:
        c.start()

    loads[0].wait()
    for r in range(16):
        tap32[r : r + 1, :] = taps_v[0:1, r * Q : (r + 1) * Q]
    tap_send[...] = tap32[...].astype(BF16)
    pl.semaphore_wait(barrier, len(peers) + len(ch_peers))
    for o in peers:
        pltpu.make_async_remote_copy(
            tap_send, tap_recv.at[p], tap_sems.at[0], tap_sems.at[1],
            device_id=(o, g), device_id_type=MESH,
        ).start()
    pltpu.make_async_copy(tap_send, tap_recv.at[p], tap_sems.at[1]).start()

    loads[1].wait()
    loads[2].wait()
    for r in range(16):
        at = pl.ds(r * Q, Q)
        prod = pre_v[:, at].astype(F32) * val_v[:, at].astype(F32)
        for q in range(4):
            sig32[q, pl.ds(r, 16, stride=16), :] = prod[:, q * 128 : (q + 1) * 128]
    for q in range(4):
        sig_send[:, :, q * 128 : (q + 1) * 128] = (
            sig32[q].astype(BF16).reshape(CHANNELS, 16, 128)
        )
    for o in peers:
        pltpu.make_async_remote_copy(
            sig_send.at[o], sig_recv.at[p], sig_sems.at[0], sig_sems.at[1],
            device_id=(o, g), device_id_type=MESH,
        ).start()
    pltpu.make_async_copy(sig_send.at[p], sig_recv.at[p], sig_sems.at[1]).start()

    for o in ch_peers:
        pltpu.make_async_remote_copy(
            post.at[:, pl.ds(pl.multiple_of(o * PIECE, PIECE), PIECE)],
            post_recv.at[g], post_sems.at[0], post_sems.at[1],
            device_id=(p, o), device_id_type=MESH,
        ).start()
    pltpu.make_async_copy(
        post.at[:, pl.ds(pl.multiple_of(g * PIECE, PIECE), PIECE)],
        post_recv.at[g], post_sems.at[1],
    ).start()

    def turned(a_re, a_im):
        t_re, t_im = tw_v[0], tw_v[1]
        return a_re * t_re - a_im * t_im, a_re * t_im + a_im * t_re

    def forward(data):
        a = jnp.dot(fwd_v[...], data, preferred_element_type=F32)
        b_re, b_im = turned(a[:R], a[R:])
        spec_b[:, :Q] = b_re.astype(BF16)
        spec_b[:, Q:] = b_im.astype(BF16)
        return jnp.dot(spec_b[...], tab_v[...], preferred_element_type=F32)

    pltpu.make_async_copy(tap_recv, tap_recv, tap_sems.at[1]).wait()
    for c in tables:
        c.wait()
    spec_h[...] = forward(tap_recv[...].reshape(R, Q))

    pltpu.make_async_copy(sig_recv, sig_recv, sig_sems.at[1]).wait()
    signal = sig_recv[...].reshape(R, Q)
    spec_z[...] = forward(signal)
    z_re, z_im = spec_z[:, :Q], spec_z[:, Q:]
    h_re, h_im = spec_h[:, :Q], spec_h[:, Q:]
    spec_b[:, :Q] = (z_re * h_re - z_im * h_im).astype(BF16)
    spec_b[:, Q:] = (-(z_re * h_im + z_im * h_re)).astype(BF16)
    u = jnp.dot(spec_b[...], tab_v[...], preferred_element_type=F32)
    v_re, v_im = turned(u[:, :Q], u[:, Q:])
    back_v[:R] = v_re.astype(BF16)
    back_v[R:] = v_im.astype(BF16)
    conv = jnp.dot(bwd_v[...], back_v[...], preferred_element_type=F32)
    total = conv + skip[p] * signal.astype(F32)
    for q in range(4):
        y32[q] = total[:, q * 128 : (q + 1) * 128]
    for e in range(2):
        for q in range(4):
            lin32[pl.ds(e * 4 + q, 128, stride=8), :] = y32[q, pl.ds(e, 128, stride=2), :]
    y_send[...] = lin32[...].reshape(128, 8, 128).astype(BF16)

    channel = g * CHANNELS + p
    me = p * CH + g

    def send_piece(k, carry):
        d = lax.rem(me + k, CTX * CH)
        pltpu.make_async_remote_copy(
            y_send.at[d], y_recv.at[channel], y_sems.at[0], y_sems.at[1],
            device_id=(d // CH, lax.rem(d, CH)), device_id_type=MESH,
        ).start()
        return carry

    lax.fori_loop(1, CTX * CH, send_piece, 0)
    pltpu.make_async_copy(y_send.at[me], y_recv.at[channel], y_sems.at[1]).start()

    pltpu.make_async_copy(post_recv, post_recv, post_sems.at[1]).wait()
    pltpu.make_async_copy(y_recv, y_recv, y_sems.at[1]).wait()
    got32[...] = y_recv[...].astype(F32).reshape(CTX * CH * 8, 128)
    for s in range(8):
        at = pl.ds(s * 128, 128)
        gate = post_recv[:, :, at].astype(F32).reshape(128, 128)
        out_v[:, at] = (got32[pl.ds(s, 128, stride=8), :] * gate).astype(BF16)
    done = pltpu.make_async_copy(out_v, out, out_sem)
    done.start()

    tail = pl.ds(0, CTX - 1)
    pltpu.make_async_copy(tap_recv.at[tail], tap_recv.at[tail], tap_sems.at[0]).wait()
    pltpu.make_async_copy(sig_send.at[tail], sig_send.at[tail], sig_sems.at[0]).wait()
    tail = pl.ds(0, CH - 1)
    pltpu.make_async_copy(post_recv.at[tail], post_recv.at[tail], post_sems.at[0]).wait()
    tail = pl.ds(0, CTX * CH - 1)
    pltpu.make_async_copy(y_send.at[tail], y_send.at[tail], y_sems.at[0]).wait()
    done.wait()


def body(pre_gate, value, post_gate, filter_taps, skip):
    fwd_t, bwd_t, tab_t, tw_t = (jnp.asarray(t) for t in build_tables())
    anyspace = pl.BlockSpec(memory_space=pl.ANY)
    vmem = pltpu.VMEM
    return pl.pallas_call(
        kernel,
        out_shape=jax.ShapeDtypeStruct((CTX * CH, PIECE), BF16),
        in_specs=[anyspace] * 4 + [pl.BlockSpec(memory_space=pltpu.SMEM)] + [anyspace] * 4,
        out_specs=anyspace,
        scratch_shapes=[
            vmem((CHANNELS, BLOCK), BF16),
            vmem((CHANNELS, BLOCK), BF16),
            vmem((1, BLOCK), F32),
            vmem((2 * R, R), BF16),
            vmem((R, 2 * R), BF16),
            vmem((2 * Q, 2 * Q), BF16),
            vmem((2, R, Q), F32),
            vmem((4, R, 128), F32),
            vmem((16, Q), F32),
            vmem((CTX, 16, Q), BF16),
            vmem((16, Q), BF16),
            vmem((CTX, 16, Q), BF16),
            vmem((CTX, 16, Q), BF16),
            vmem((CH, CHANNELS, PIECE), BF16),
            vmem((R, 2 * Q), BF16),
            vmem((R, 2 * Q), F32),
            vmem((R, 2 * Q), F32),
            vmem((2 * R, Q), BF16),
            vmem((4, R, 128), F32),
            vmem((CTX * CH * 8, 128), F32),
            vmem((CTX * CH, 8, 128), BF16),
            vmem((CTX * CH, 8, 128), BF16),
            vmem((CTX * CH * 8, 128), F32),
            vmem((CTX * CH, PIECE), BF16),
            pltpu.SemaphoreType.DMA((3,)),
            pltpu.SemaphoreType.DMA((4,)),
            pltpu.SemaphoreType.DMA((2,)),
            pltpu.SemaphoreType.DMA((2,)),
            pltpu.SemaphoreType.DMA((2,)),
            pltpu.SemaphoreType.DMA((2,)),
            pltpu.SemaphoreType.DMA,
        ],
        compiler_params=pltpu.CompilerParams(
            collective_id=0, has_side_effects=True, vmem_limit_bytes=56 * 1024 * 1024
        ),
        name="hyena",
    )(pre_gate, value, post_gate, filter_taps, skip, fwd_t, bwd_t, tab_t, tw_t)


def solution(mesh):
    placed = (P("ch", "ctx"), P("ch", "ctx"), P("ch", "ctx"), P("ch", "ctx"), P("ch"))
    return jax.shard_map(
        body, mesh=mesh, in_specs=placed, out_specs=P(None, ("ctx", "ch")), check_vma=False
    )
```

profile of v0, /device:TPU:1, one launch (start us, length us, event | category | flops | bytes accessed | tf_op | source)
XLA Modules:
  0.0 29.7 jit_solution(11371823144692354817)
XLA Ops:
  0.0 28.1 %hyena.1 = bf16[128,1024]{1,0:T(8,128)(2,1)} custom-call(bf16[16,8192]{1,0:T(8,128)(2,1)} %pre.1, bf16[16,8192]{1,0:T(8,128)(2,1)} %val.1, bf16[16,8192]{1,0:T(8,128)(2,1)} %post.1, f32[1,8192]{1,0:T(1,128)} %taps.1, f32[16]{0:T(128)} %skip.1, bf16[512,256]{1,0:T(8,128)(2,1)} %constant.8.clone.fwd_t, bf16[256,512]{1,0:T(8,128)(2,1)} %constant.9.clone.bwd_t, ...), custom_call_target="tpu_custom_call" | custom-call | tf_op jit(solution)/shard_map/hyena/pallas_call | solution.py:193
  28.1 1.7 %copy.11 = bf16[128,1024]{1,0:T(8,128)(2,1)} copy(bf16[128,1024]{1,0:T(8,128)(2,1)} %hyena.1) | data formatting | bytes 524288
where the time goes:
time: 29.9 us; the launch traced here: 29.7 us
  Pallas kernels  28.1 us (94%)
  local copies, waits for them, and re-layouts  1.67 us (6%)
    pallas_call x1, Pallas kernels, body(): pl.pallas_call(kernel, out_shape=jax.ShapeDtypeStruct((CTX * CH, PIECE),...  28.1 us
    unnamed x1, local copies, waits for them, and re-layouts  1.67 us

commit v1 on v0

v1 whole, which is shorter than its diff:
```python
import jax
import jax.numpy as jnp
import numpy as np
import ml_dtypes
from jax import lax
from jax.experimental import pallas as pl
from jax.experimental.pallas import tpu as pltpu
from jax.sharding import PartitionSpec as P

MESH = pl.DeviceIdType.MESH
F32 = jnp.float32
BF16 = jnp.bfloat16

CTX_Y = 4
CTX = 16
CH = 8
HALF = 8
CHANNELS = 16
BLOCK = 8192
R = 256
Q = 512
PIECE = 1024


def ring(step):
    return min(step, 4 - step)


FAR_FIRST = sorted(
    [
        (dx, dy, dz, dc)
        for dx in range(4)
        for dy in range(4)
        for dz in range(4)
        for dc in range(2)
        if dx or dy or dz or dc
    ],
    key=lambda o: -(ring(o[0]) + ring(o[1]) + ring(o[2])),
)


def build_tables():
    rows = np.arange(R)
    cols = np.arange(Q)
    first = 2 * np.pi * ((np.outer(2 * rows + 1, rows)) % 1024) / 1024.0
    forward = np.concatenate([np.cos(first), -np.sin(first)], axis=0)
    backward = np.concatenate([np.cos(first).T, np.sin(first).T], axis=1) * (2.0**-17)
    turn = 2 * np.pi * np.outer(2 * rows + 1, cols) / 2.0**19
    twiddle = np.stack([np.cos(turn), -np.sin(turn)])
    second = 2 * np.pi * (np.outer(cols, cols) % Q) / Q
    wr, wi = np.cos(second), -np.sin(second)
    table = np.concatenate([np.concatenate([wr, wi], 1), np.concatenate([-wi, wr], 1)], 0)
    half = lambda a: a.astype(np.float32).astype(ml_dtypes.bfloat16)
    return half(forward), half(backward), half(table), twiddle.astype(np.float32)


def kernel(
    pre, val, post, taps, skip_hbm, fwd_t, bwd_t, tab_t, tw_t, y_out, post_out,
    pre_v, val_v, taps_v, fwd_v, bwd_v, tab_v, tw_v,
    sig32, tap32, sig_send, tap_send, sig_recv, tap_recv, skip_send, skip_recv,
    spec_b, spec_z, spec_h, back_v, y32, lin32, y_send,
    skip, load_sems, table_sems, sig_sems, tap_sems, pass_sems, skip_sems, post_sems, y_sems,
):
    p = lax.axis_index("ctx")
    g = lax.axis_index("ch")
    px, py = p // CTX_Y, p % CTX_Y
    z, core = g // 2, g % 2
    xs = [(px + i) % 4 for i in range(4)]
    ys = [(py + i) % 4 for i in range(4)]
    zs = [(z + i) % 4 for i in range(4)]
    cs = [core, 1 - core]
    sibling = z * 2 + 1 - core
    half = p // HALF
    at_home = half == core
    own_group = z * 2 + half
    own_channel = (p % HALF) * 2 + core

    near_x = 2 * core + lax.rem(px, 2)
    flip_x = 2 * core + 1 - lax.rem(px, 2)
    first_x = jnp.where(at_home, flip_x, near_x)
    last_x = jnp.where(at_home, near_x, flip_x)
    workers = [
        first_x * CTX_Y + ys[2], first_x * CTX_Y + ys[1], first_x * CTX_Y + ys[3], last_x * CTX_Y + ys[2],
        last_x * CTX_Y + ys[1], last_x * CTX_Y + ys[3], first_x * CTX_Y + ys[0], last_x * CTX_Y + ys[0],
    ]

    barrier = pltpu.get_barrier_semaphore()
    for dx in (2, 1, 3, 0):
        for dy in (2, 1, 3, 0):
            if dx or dy:
                pl.semaphore_signal(
                    barrier, inc=1, device_id=(xs[dx] * CTX_Y + ys[dy], z * 2 + half), device_id_type=MESH
                )
    for dz, dc in ((2, 0), (2, 1), (1, 0), (3, 0), (1, 1), (3, 1), (0, 1)):
        pl.semaphore_signal(barrier, inc=1, device_id=(p, zs[dz] * 2 + cs[dc]), device_id_type=MESH)

    loads = [
        pltpu.make_async_copy(a, b, load_sems.at[i])
        for i, (a, b) in enumerate([(taps, taps_v), (pre, pre_v), (val, val_v), (skip_hbm, skip)])
    ]
    tables = [
        pltpu.make_async_copy(a, b, table_sems.at[i])
        for i, (a, b) in enumerate([(fwd_t, fwd_v), (tw_t, tw_v), (tab_t, tab_v), (bwd_t, bwd_v)])
    ]
    for c in loads + tables:
        c.start()

    loads[0].wait()
    for r in range(16):
        tap32[r : r + 1, :] = taps_v[0:1, r * Q : (r + 1) * Q]
    tap_send[...] = tap32[...].astype(BF16)
    loads[1].wait()
    loads[2].wait()
    for r in range(16):
        at = pl.ds(r * Q, Q)
        prod = pre_v[:, at].astype(F32) * val_v[:, at].astype(F32)
        for q in range(4):
            sig32[q, pl.ds(r, 16, stride=16), :] = prod[:, q * 128 : (q + 1) * 128]
    for q in range(4):
        sig_send[:, :, q * 128 : (q + 1) * 128] = (
            sig32[q].astype(BF16).reshape(CHANNELS, 16, 128)
        )

    @pl.when(at_home)
    def _():
        pl.semaphore_wait(barrier, 7 + 14)

    @pl.when(jnp.logical_not(at_home))
    def _():
        pl.semaphore_wait(barrier, 7 + 16)

    def send_taps(o):
        pltpu.make_async_remote_copy(
            tap_send, tap_recv.at[p], tap_sems.at[0], tap_sems.at[1],
            device_id=(o, z * 2 + half), device_id_type=MESH,
        ).start()

    def send_signal(o, k):
        pltpu.make_async_remote_copy(
            sig_send.at[lax.rem(o, HALF) * 2 + k], sig_recv.at[p], sig_sems.at[0], sig_sems.at[1],
            device_id=(o, z * 2 + k), device_id_type=MESH,
        ).start()

    for o in workers[:-1]:
        send_taps(o)
    for o in workers[:-1]:
        send_signal(o, 0)
        send_signal(o, 1)
    far = workers[-1]

    @pl.when(at_home)
    def _():
        pltpu.make_async_copy(tap_send, tap_recv.at[p], tap_sems.at[1]).start()
        pltpu.make_async_remote_copy(
            sig_send.at[lax.rem(p, HALF) * 2 + 1 - core], sig_recv.at[p], sig_sems.at[0], sig_sems.at[1],
            device_id=(p, sibling), device_id_type=MESH,
        ).start()
        pltpu.make_async_copy(sig_send.at[own_channel], sig_recv.at[p], sig_sems.at[1]).start()

    @pl.when(jnp.logical_not(at_home))
    def _():
        send_taps(far)
        send_signal(far, 0)
        send_signal(far, 1)

    loads[3].wait()
    skip_send[...] = jnp.full((8, 128), skip[(p % HALF) * 2 + 1 - core], F32)
    to_sibling = pltpu.make_async_remote_copy(
        skip_send, skip_recv, skip_sems.at[0], skip_sems.at[1],
        device_id=(p, sibling), device_id_type=MESH,
    )
    to_sibling.start()

    def post_part(o):
        return post.at[:, pl.ds(pl.multiple_of(o * PIECE, PIECE), PIECE)]

    for dz, dc in ((2, 0), (2, 1), (1, 0), (3, 0), (1, 1), (3, 1), (0, 1)):
        o = zs[dz] * 2 + cs[dc]
        pltpu.make_async_remote_copy(
            post_part(o), post_out.at[g], post_sems.at[0], post_sems.at[1],
            device_id=(p, o), device_id_type=MESH,
        ).start()
    pltpu.make_async_copy(post_part(g), post_out.at[g], post_sems.at[1]).start()

    mine = tap_recv.at[pl.ds(core * HALF, HALF)]
    theirs = tap_recv.at[pl.ds((1 - core) * HALF, HALF)]
    pltpu.make_async_copy(mine, mine, tap_sems.at[1]).wait()
    passed = pltpu.make_async_remote_copy(
        mine, mine, pass_sems.at[0], pass_sems.at[1], device_id=(p, sibling), device_id_type=MESH
    )
    passed.start()

    def turned(a_re, a_im):
        t_re, t_im = tw_v[0], tw_v[1]
        return a_re * t_re - a_im * t_im, a_re * t_im + a_im * t_re

    def forward(data):
        a = jnp.dot(fwd_v[...], data, preferred_element_type=F32)
        b_re, b_im = turned(a[:R], a[R:])
        spec_b[:, :Q] = b_re.astype(BF16)
        spec_b[:, Q:] = b_im.astype(BF16)
        return jnp.dot(spec_b[...], tab_v[...], preferred_element_type=F32)

    for c in tables:
        c.wait()
    pltpu.make_async_copy(theirs, theirs, pass_sems.at[1]).wait()
    spec_h[...] = forward(tap_recv[...].reshape(R, Q))

    pltpu.make_async_copy(sig_recv, sig_recv, sig_sems.at[1]).wait()
    signal = sig_recv[...].reshape(R, Q)
    spec_z[...] = forward(signal)
    z_re, z_im = spec_z[:, :Q], spec_z[:, Q:]
    h_re, h_im = spec_h[:, :Q], spec_h[:, Q:]
    spec_b[:, :Q] = (z_re * h_re - z_im * h_im).astype(BF16)
    spec_b[:, Q:] = (-(z_re * h_im + z_im * h_re)).astype(BF16)
    u = jnp.dot(spec_b[...], tab_v[...], preferred_element_type=F32)
    v_re, v_im = turned(u[:, :Q], u[:, Q:])
    back_v[:R] = v_re.astype(BF16)
    back_v[R:] = v_im.astype(BF16)
    conv = jnp.dot(bwd_v[...], back_v[...], preferred_element_type=F32)
    to_sibling.wait_recv()
    weight = jnp.where(at_home, skip[own_channel], skip_recv[0:1, :])
    for q in range(4):
        at = slice(q * 128, (q + 1) * 128)
        y32[q] = conv[:, at] + weight * signal[:, at].astype(F32)
    for e in range(2):
        for q in range(4):
            lin32[pl.ds(e * 4 + q, 128, stride=8), :] = y32[q, pl.ds(e, 128, stride=2), :]
    y_send[...] = lin32[...].reshape(CTX * CH, 8, 128).astype(BF16)

    channel = own_group * CHANNELS + own_channel
    for dx, dy, dz, dc in FAR_FIRST:
        o_ctx = xs[dx] * CTX_Y + ys[dy]
        o_ch = zs[dz] * 2 + cs[dc]
        pltpu.make_async_remote_copy(
            y_send.at[o_ctx * CH + o_ch], y_out.at[channel], y_sems.at[0], y_sems.at[1],
            device_id=(o_ctx, o_ch), device_id_type=MESH,
        ).start()
    pltpu.make_async_copy(y_send.at[p * CH + g], y_out.at[channel], y_sems.at[1]).start()

    @pl.when(at_home)
    def _():
        part = sig_send.at[pl.ds(0, 15)]
        pltpu.make_async_copy(part, part, sig_sems.at[0]).wait()
        part = tap_recv.at[pl.ds(0, 7)]
        pltpu.make_async_copy(part, part, tap_sems.at[0]).wait()

    @pl.when(jnp.logical_not(at_home))
    def _():
        pltpu.make_async_copy(sig_send, sig_send, sig_sems.at[0]).wait()
        part = tap_recv.at[pl.ds(0, 8)]
        pltpu.make_async_copy(part, part, tap_sems.at[0]).wait()

    passed.wait_send()
    to_sibling.wait_send()
    part = post_out.at[pl.ds(0, CH - 1)]
    pltpu.make_async_copy(part, part, post_sems.at[0]).wait()
    pltpu.make_async_copy(post_out, post_out, post_sems.at[1]).wait()
    part = y_send.at[pl.ds(0, CTX * CH - 1)]
    pltpu.make_async_copy(part, part, y_sems.at[0]).wait()
    pltpu.make_async_copy(y_out, y_out, y_sems.at[1]).wait()


def gate_kernel(y, post, out, wide):
    wide[...] = y[...].astype(F32).reshape(wide.shape)
    rows = out.shape[0]
    for s in range(8):
        at = pl.ds(s * 128, 128)
        gate = post[:, at].astype(F32)
        out[:, at] = (wide[pl.ds(s, rows, stride=8), :] * gate).astype(BF16)


def body(pre_gate, value, post_gate, filter_taps, skip):
    fwd_t, bwd_t, tab_t, tw_t = (jnp.asarray(t) for t in build_tables())
    anyspace = pl.BlockSpec(memory_space=pl.ANY)
    vmem = pltpu.VMEM
    dma = pltpu.SemaphoreType.DMA
    whole = pl.BlockSpec(memory_space=vmem)
    conv, gate = pl.pallas_call(
        kernel,
        out_shape=[
            vmem((CTX * CH, 8, 128), BF16),
            vmem((CH, CHANNELS, PIECE), BF16),
        ],
        in_specs=[anyspace] * 9,
        out_specs=[whole, whole],
        scratch_shapes=[
            vmem((CHANNELS, BLOCK), BF16),
            vmem((CHANNELS, BLOCK), BF16),
            vmem((1, BLOCK), F32),
            vmem((2 * R, R), BF16),
            vmem((R, 2 * R), BF16),
            vmem((2 * Q, 2 * Q), BF16),
            vmem((2, R, Q), F32),
            vmem((4, R, 128), F32),
            vmem((16, Q), F32),
            vmem((CTX, 16, Q), BF16),
            vmem((16, Q), BF16),
            vmem((CTX, 16, Q), BF16),
            vmem((CTX, 16, Q), BF16),
            vmem((8, 128), F32),
            vmem((8, 128), F32),
            vmem((R, 2 * Q), BF16),
            vmem((R, 2 * Q), F32),
            vmem((R, 2 * Q), F32),
            vmem((2 * R, Q), BF16),
            vmem((4, R, 128), F32),
            vmem((CTX * CH * 8, 128), F32),
            vmem((CTX * CH, 8, 128), BF16),
            pltpu.SMEM((16,), F32),
            dma((4,)),
            dma((4,)),
            dma((2,)),
            dma((2,)),
            dma((2,)),
            dma((2,)),
            dma((2,)),
            dma((2,)),
        ],
        compiler_params=pltpu.CompilerParams(
            collective_id=0, has_side_effects=True, vmem_limit_bytes=56 * 1024 * 1024
        ),
        name="hyena",
    )(pre_gate, value, post_gate, filter_taps, skip, fwd_t, bwd_t, tab_t, tw_t)
    return pl.pallas_call(
        gate_kernel,
        out_shape=jax.ShapeDtypeStruct((CTX * CH, PIECE), BF16),
        in_specs=[whole, whole],
        out_specs=whole,
        scratch_shapes=[vmem((CTX * CH * 8, 128), F32)],
        compiler_params=pltpu.CompilerParams(vmem_limit_bytes=4 * 1024 * 1024),
        name="gate",
    )(conv, gate.reshape(CTX * CH, PIECE))


def solution(mesh):
    placed = (P("ch", "ctx"), P("ch", "ctx"), P("ch", "ctx"), P("ch", "ctx"), P("ch"))
    return jax.shard_map(
        body, mesh=mesh, in_specs=placed, out_specs=P(None, ("ctx", "ch")), check_vma=False
    )
```

time: 29.9 us -> 26.1 us (0.87)
  Pallas kernels: 28.1 us -> 26 us
  local copies, waits for them, and re-layouts: 1.67 us -> 0 us
    pallas_call x1 -> x2, Pallas kernels: 28.1 us -> 26 us  [the longest x1 25.2 us: body(): pl.pallas_call(kernel, out_shape=[vmem((CTX * CH, 8, 128), BF16), vmem((C...]
    unnamed x1 -> x0, local copies, waits for them, and re-layouts: 1.67 us -> none
where the time goes in v1:
time: 26.1 us; the launch traced here: 26 us
  Pallas kernels  26 us (100%)
    pallas_call x1, Pallas kernels, body(): pl.pallas_call(kernel, out_shape=[vmem((CTX * CH, 8, 128), BF16), vmem((C...  25.2 us
    pallas_call x1, Pallas kernels, body(): pl.pallas_call(gate_kernel, out_shape=jax.ShapeDtypeStruct((CTX * CH, PIE...  0.87 us

profile of v1, /device:TPU:1, one launch (start us, length us, event | category | flops | bytes accessed | tf_op | source)
XLA Modules:
  0.0 26.0 jit_solution(8298749180169900049)
XLA Ops:
  0.0 25.2 %hyena.1 = (bf16[128,8,128]{2,1,0:T(8,128)(2,1)S(1)}, bf16[8,16,1024]{2,1,0:T(8,128)(2,1)S(1)}) custom-call(bf16[16,8192]{1,0:T(8,128)(2,1)} %pre.1, bf16[16,8192]{1,0:T(8,128)(2,1)} %val.1, bf16[16,8192]{1,0:T(8,128)(2,1)} %post.1, f32[1,8192]{1,0:T(1,128)} %taps.1, f32[16]{0:T(128)} %skip_hbm.1, bf16[512,256]{1,0:T(8,128)(2,1)} %constant.8.clone.fwd_t, ...), custom_call_target="tpu_custom_call" | custom-call | tf_op jit(solution)/shard_map/hyena/pallas_call | solution.py:279
  25.2 0.9 %gate.1 = bf16[128,1024]{1,0:T(8,128)(2,1)} custom-call(bf16[128,8,128]{2,1,0:T(8,128)(2,1)S(1)} %get-tuple-element.7.y, bf16[128,1024]{1,0:T(8,128)(2,1)S(1)} %bitcast.1), custom_call_target="tpu_custom_call" | custom-call | tf_op jit(solution)/shard_map/gate/pallas_call | solution.py:325

commit v2 on v1

--- a/solution.py
+++ b/solution.py
@@ -39,26 +39,44 @@
 )
 
 
+def pair(table, flip):
+    re, im = table.real, table.imag
+    return np.block([[re, im], [im, -re]]) if flip else np.block([[re, im], [-im, re]])
+
+
 def build_tables():
     rows = np.arange(R)
     cols = np.arange(Q)
+    part = np.arange(128)
     first = 2 * np.pi * ((np.outer(2 * rows + 1, rows)) % 1024) / 1024.0
     forward = np.concatenate([np.cos(first), -np.sin(first)], axis=0)
-    backward = np.concatenate([np.cos(first).T, np.sin(first).T], axis=1) * (2.0**-17)
+    order = np.concatenate([rows[0::2], rows[1::2]])
+    backward = np.concatenate([np.cos(first).T, np.sin(first).T], axis=1)[order] * (2.0**-17)
     turn = 2 * np.pi * np.outer(2 * rows + 1, cols) / 2.0**19
     twiddle = np.stack([np.cos(turn), -np.sin(turn)])
-    second = 2 * np.pi * (np.outer(cols, cols) % Q) / Q
-    wr, wi = np.cos(second), -np.sin(second)
-    table = np.concatenate([np.concatenate([wr, wi], 1), np.concatenate([-wi, wr], 1)], 0)
+    waves = [np.exp(-2j * np.pi * (np.outer(part, d + 4 * part) % Q) / Q) for d in range(4)]
+    there = np.concatenate([pair(w, False) for w in waves], axis=0)
+    back = np.concatenate([pair(w.T, True) for w in waves], axis=0)
     half = lambda a: a.astype(np.float32).astype(ml_dtypes.bfloat16)
-    return half(forward), half(backward), half(table), twiddle.astype(np.float32)
+    return half(forward), half(backward), half(there), half(back), twiddle.astype(np.float32)
+
+
+def times(a, b):
+    return a[0] * b[0] - a[1] * b[1], a[0] * b[1] + a[1] * b[0]
+
+
+def four_point(v):
+    (r0, i0), (r1, i1), (r2, i2), (r3, i3) = v
+    sr, si, dr, di = r0 + r2, i0 + i2, r0 - r2, i0 - i2
+    ur, ui, er, ei = r1 + r3, i1 + i3, r1 - r3, i1 - i3
+    return [(sr + ur, si + ui), (dr + ei, di - er), (sr - ur, si - ui), (dr - ei, di + er)]
 
 
 def kernel(
-    pre, val, post, taps, skip_hbm, fwd_t, bwd_t, tab_t, tw_t, y_out, post_out,
-    pre_v, val_v, taps_v, fwd_v, bwd_v, tab_v, tw_v,
+    pre, val, post, taps, skip_hbm, fwd_t, bwd_t, there_t, back_t, tw_t, y_out, post_out,
+    pre_v, val_v, taps_v, fwd_v, bwd_v, there_v, back_v, tw_v,
     sig32, tap32, sig_send, tap_send, sig_recv, tap_recv, skip_send, skip_recv,
-    spec_b, spec_z, spec_h, back_v, y32, lin32, y_send,
+    spec_h, y32, lin32, y_send,
     skip, load_sems, table_sems, sig_sems, tap_sems, pass_sems, skip_sems, post_sems, y_sems,
 ):
     p = lax.axis_index("ctx")
@@ -100,7 +118,7 @@
     ]
     tables = [
         pltpu.make_async_copy(a, b, table_sems.at[i])
-        for i, (a, b) in enumerate([(fwd_t, fwd_v), (tw_t, tw_v), (tab_t, tab_v), (bwd_t, bwd_v)])
+        for i, (a, b) in enumerate([(fwd_t, fwd_v), (tw_t, tw_v), (there_t, there_v), (back_t, back_v), (bwd_t, bwd_v)])
     ]
     for c in loads + tables:
         c.start()
@@ -190,42 +208,50 @@
     )
     passed.start()
 
-    def turned(a_re, a_im):
-        t_re, t_im = tw_v[0], tw_v[1]
-        return a_re * t_re - a_im * t_im, a_re * t_im + a_im * t_re
-
-    def forward(data):
+    def lanes(a):
+        return slice(a * 128, (a + 1) * 128)
+
+    def turn(a):
+        return tw_v[0, :, lanes(a)], tw_v[1, :, lanes(a)]
+
+    def joined(re, im):
+        return jnp.concatenate([re.astype(BF16), im.astype(BF16)], axis=1)
+
+    def spectrum(data):
         a = jnp.dot(fwd_v[...], data, preferred_element_type=F32)
-        b_re, b_im = turned(a[:R], a[R:])
-        spec_b[:, :Q] = b_re.astype(BF16)
-        spec_b[:, Q:] = b_im.astype(BF16)
-        return jnp.dot(spec_b[...], tab_v[...], preferred_element_type=F32)
+        parts = four_point([times((a[:R, lanes(i)], a[R:, lanes(i)]), turn(i)) for i in range(4)])
+        return [
+            jnp.dot(joined(*parts[d]), there_v[d * R : (d + 1) * R, :], preferred_element_type=F32)
+            for d in range(4)
+        ]
 
     for c in tables:
         c.wait()
     pltpu.make_async_copy(theirs, theirs, pass_sems.at[1]).wait()
-    spec_h[...] = forward(tap_recv[...].reshape(R, Q))
+    for d, part in enumerate(spectrum(tap_recv[...].reshape(R, Q))):
+        spec_h[d] = part
 
     pltpu.make_async_copy(sig_recv, sig_recv, sig_sems.at[1]).wait()
     signal = sig_recv[...].reshape(R, Q)
-    spec_z[...] = forward(signal)
-    z_re, z_im = spec_z[:, :Q], spec_z[:, Q:]
-    h_re, h_im = spec_h[:, :Q], spec_h[:, Q:]
-    spec_b[:, :Q] = (z_re * h_re - z_im * h_im).astype(BF16)
-    spec_b[:, Q:] = (-(z_re * h_im + z_im * h_re)).astype(BF16)
-    u = jnp.dot(spec_b[...], tab_v[...], preferred_element_type=F32)
-    v_re, v_im = turned(u[:, :Q], u[:, Q:])
-    back_v[:R] = v_re.astype(BF16)
-    back_v[R:] = v_im.astype(BF16)
-    conv = jnp.dot(bwd_v[...], back_v[...], preferred_element_type=F32)
     to_sibling.wait_recv()
     weight = jnp.where(at_home, skip[own_channel], skip_recv[0:1, :])
     for q in range(4):
-        at = slice(q * 128, (q + 1) * 128)
-        y32[q] = conv[:, at] + weight * signal[:, at].astype(F32)
+        y32[q] = weight * signal[:, lanes(q)].astype(F32)
+    parts = []
+    for d, part in enumerate(spectrum(signal)):
+        prod = times((part[:, :128], part[:, 128:]), (spec_h[d, :, :128], spec_h[d, :, 128:]))
+        part = jnp.dot(joined(*prod), back_v[d * R : (d + 1) * R, :], preferred_element_type=F32)
+        parts.append((part[:, :128], part[:, 128:]))
+    parts = [times(part, turn(i)) for i, part in enumerate(four_point(parts))]
+    columns = jnp.concatenate(
+        [jnp.concatenate([part[i].astype(BF16) for part in parts], axis=1) for i in range(2)], axis=0
+    )
+    conv = jnp.dot(bwd_v[...], columns, preferred_element_type=F32)
     for e in range(2):
         for q in range(4):
-            lin32[pl.ds(e * 4 + q, 128, stride=8), :] = y32[q, pl.ds(e, 128, stride=2), :]
+            lin32[pl.ds(e * 4 + q, 128, stride=8), :] = (
+                conv[e * 128 : (e + 1) * 128, lanes(q)] + y32[q, pl.ds(e, 128, stride=2), :]
+            )
     y_send[...] = lin32[...].reshape(CTX * CH, 8, 128).astype(BF16)
 
     channel = own_group * CHANNELS + own_channel
@@ -271,7 +297,7 @@
 
 
 def body(pre_gate, value, post_gate, filter_taps, skip):
-    fwd_t, bwd_t, tab_t, tw_t = (jnp.asarray(t) for t in build_tables())
+    tables = tuple(jnp.asarray(t) for t in build_tables())
     anyspace = pl.BlockSpec(memory_space=pl.ANY)
     vmem = pltpu.VMEM
     dma = pltpu.SemaphoreType.DMA
@@ -282,7 +308,7 @@
             vmem((CTX * CH, 8, 128), BF16),
             vmem((CH, CHANNELS, PIECE), BF16),
         ],
-        in_specs=[anyspace] * 9,
+        in_specs=[anyspace] * 10,
         out_specs=[whole, whole],
         scratch_shapes=[
             vmem((CHANNELS, BLOCK), BF16),
@@ -290,7 +316,8 @@
             vmem((1, BLOCK), F32),
             vmem((2 * R, R), BF16),
             vmem((R, 2 * R), BF16),
-            vmem((2 * Q, 2 * Q), BF16),
+            vmem((4 * R, R), BF16),
+            vmem((4 * R, R), BF16),
             vmem((2, R, Q), F32),
             vmem((4, R, 128), F32),
             vmem((16, Q), F32),
@@ -300,16 +327,13 @@
             vmem((CTX, 16, Q), BF16),
             vmem((8, 128), F32),
             vmem((8, 128), F32),
-            vmem((R, 2 * Q), BF16),
-            vmem((R, 2 * Q), F32),
-            vmem((R, 2 * Q), F32),
-            vmem((2 * R, Q), BF16),
+            vmem((4, R, 2 * 128), F32),
             vmem((4, R, 128), F32),
             vmem((CTX * CH * 8, 128), F32),
             vmem((CTX * CH, 8, 128), BF16),
             pltpu.SMEM((16,), F32),
             dma((4,)),
-            dma((4,)),
+            dma((5,)),
             dma((2,)),
             dma((2,)),
             dma((2,)),
@@ -321,7 +345,7 @@
             collective_id=0, has_side_effects=True, vmem_limit_bytes=56 * 1024 * 1024
         ),
         name="hyena",
-    )(pre_gate, value, post_gate, filter_taps, skip, fwd_t, bwd_t, tab_t, tw_t)
+    )(pre_gate, value, post_gate, filter_taps, skip, *tables)
     return pl.pallas_call(
         gate_kernel,
         out_shape=jax.ShapeDtypeStruct((CTX * CH, PIECE), BF16),

time: 26.1 us -> 25.3 us (0.969)
  Pallas kernels: 26 us -> 25.2 us
    pallas_call x1, Pallas kernels: 25.2 us -> 24.3 us  [body(): pl.pallas_call(kernel, out_shape=[vmem((CTX * CH, 8, 128), BF16), vmem((C...]
where the time goes in v2:
time: 25.3 us; the launch traced here: 25.2 us
  Pallas kernels  25.2 us (100%)
    pallas_call x1, Pallas kernels, body(): pl.pallas_call(kernel, out_shape=[vmem((CTX * CH, 8, 128), BF16), vmem((C...  24.3 us
    pallas_call x1, Pallas kernels, body(): pl.pallas_call(gate_kernel, out_shape=jax.ShapeDtypeStruct((CTX * CH, PIE...  0.87 us

profile of v2, /device:TPU:1, one launch (start us, length us, event | category | flops | bytes accessed | tf_op | source)
XLA Modules:
  0.0 25.2 jit_solution(4034242499907279881)
XLA Ops:
  0.0 24.3 %hyena.1 = (bf16[128,8,128]{2,1,0:T(8,128)(2,1)S(1)}, bf16[8,16,1024]{2,1,0:T(8,128)(2,1)S(1)}) custom-call(bf16[16,8192]{1,0:T(8,128)(2,1)} %pre.1, bf16[16,8192]{1,0:T(8,128)(2,1)} %val.1, bf16[16,8192]{1,0:T(8,128)(2,1)} %post.1, f32[1,8192]{1,0:T(1,128)} %taps.1, f32[16]{0:T(128)} %skip_hbm.1, bf16[512,256]{1,0:T(8,128)(2,1)} %constant.10.clone.fwd_t, ...), custom_call_target="tpu_custom_call" | custom-call | tf_op jit(solution)/shard_map/hyena/pallas_call | solution.py:305
  24.3 0.9 %gate.1 = bf16[128,1024]{1,0:T(8,128)(2,1)} custom-call(bf16[128,8,128]{2,1,0:T(8,128)(2,1)S(1)} %get-tuple-element.7.y, bf16[128,1024]{1,0:T(8,128)(2,1)S(1)} %bitcast.1), custom_call_target="tpu_custom_call" | custom-call | tf_op jit(solution)/shard_map/gate/pallas_call | solution.py:349

commit v3 on v2

--- a/solution.py
+++ b/solution.py
@@ -27,14 +27,7 @@
 
 
 FAR_FIRST = sorted(
-    [
-        (dx, dy, dz, dc)
-        for dx in range(4)
-        for dy in range(4)
-        for dz in range(4)
-        for dc in range(2)
-        if dx or dy or dz or dc
-    ],
+    [(dx, dy, dz) for dx in range(4) for dy in range(4) for dz in range(4)],
     key=lambda o: -(ring(o[0]) + ring(o[1]) + ring(o[2])),
 )
 
@@ -255,13 +248,26 @@
     y_send[...] = lin32[...].reshape(CTX * CH, 8, 128).astype(BF16)
 
     channel = own_group * CHANNELS + own_channel
-    for dx, dy, dz, dc in FAR_FIRST:
-        o_ctx = xs[dx] * CTX_Y + ys[dy]
-        o_ch = zs[dz] * 2 + cs[dc]
+    def send_piece(o_ctx, o_ch):
         pltpu.make_async_remote_copy(
             y_send.at[o_ctx * CH + o_ch], y_out.at[channel], y_sems.at[0], y_sems.at[1],
             device_id=(o_ctx, o_ch), device_id_type=MESH,
         ).start()
+
+    for o_ch in (1, 0):
+
+        @pl.when(jnp.logical_or(p != 0, g != o_ch))
+        def _(o_ch=o_ch):
+            send_piece(0, o_ch)
+
+    for dx, dy, dz in FAR_FIRST:
+        o_ctx = xs[dx] * CTX_Y + ys[dy]
+
+        @pl.when(o_ctx + zs[dz] != 0)
+        def _(o_ctx=o_ctx, dx=dx, dy=dy, dz=dz):
+            for dc in (0, 1) if dx or dy or dz else (1,):
+                send_piece(o_ctx, zs[dz] * 2 + cs[dc])
+
     pltpu.make_async_copy(y_send.at[p * CH + g], y_out.at[channel], y_sems.at[1]).start()
 
     @pl.when(at_home)

time: 25.3 us -> 24.2 us (0.957)
  Pallas kernels: 25.2 us -> 24.1 us
    pallas_call x1, Pallas kernels: 24.3 us -> 23.2 us  [body(): pl.pallas_call(kernel, out_shape=[vmem((CTX * CH, 8, 128), BF16), vmem((C...]
where the time goes in v3:
time: 24.2 us; the launch traced here: 24.1 us
  Pallas kernels  24.1 us (100%)
    pallas_call x1, Pallas kernels, body(): pl.pallas_call(kernel, out_shape=[vmem((CTX * CH, 8, 128), BF16), vmem((C...  23.2 us
    pallas_call x1, Pallas kernels, body(): pl.pallas_call(gate_kernel, out_shape=jax.ShapeDtypeStruct((CTX * CH, PIE...  0.87 us

profile of v3, /device:TPU:1, one launch (start us, length us, event | category | flops | bytes accessed | tf_op | source)
XLA Modules:
  0.0 24.1 jit_solution(2916188873364713555)
XLA Ops:
  0.0 23.2 %hyena.1 = (bf16[128,8,128]{2,1,0:T(8,128)(2,1)S(1)}, bf16[8,16,1024]{2,1,0:T(8,128)(2,1)S(1)}) custom-call(bf16[16,8192]{1,0:T(8,128)(2,1)} %pre.1, bf16[16,8192]{1,0:T(8,128)(2,1)} %val.1, bf16[16,8192]{1,0:T(8,128)(2,1)} %post.1, f32[1,8192]{1,0:T(1,128)} %taps.1, f32[16]{0:T(128)} %skip_hbm.1, bf16[512,256]{1,0:T(8,128)(2,1)} %constant.10.clone.fwd_t, ...), custom_call_target="tpu_custom_call" | custom-call | tf_op jit(solution)/shard_map/hyena/pallas_call | solution.py:311
  23.2 0.9 %gate.1 = bf16[128,1024]{1,0:T(8,128)(2,1)} custom-call(bf16[128,8,128]{2,1,0:T(8,128)(2,1)S(1)} %get-tuple-element.7.y, bf16[128,1024]{1,0:T(8,128)(2,1)S(1)} %bitcast.1), custom_call_target="tpu_custom_call" | custom-call | tf_op jit(solution)/shard_map/gate/pallas_call | solution.py:355

commit v4 on v3

--- a/solution.py
+++ b/solution.py
@@ -19,6 +19,7 @@
 BLOCK = 8192
 R = 256
 Q = 512
+GATE_PARTS = 4
 PIECE = 1024
 
 
@@ -26,10 +27,7 @@
     return min(step, 4 - step)
 
 
-FAR_FIRST = sorted(
-    [(dx, dy, dz) for dx in range(4) for dy in range(4) for dz in range(4)],
-    key=lambda o: -(ring(o[0]) + ring(o[1]) + ring(o[2])),
-)
+FAR_FIRST = sorted([(dx, dy) for dx in range(4) for dy in range(4)], key=lambda o: -(ring(o[0]) + ring(o[1])))
 
 
 def pair(table, flip):
@@ -81,18 +79,20 @@
     zs = [(z + i) % 4 for i in range(4)]
     cs = [core, 1 - core]
     sibling = z * 2 + 1 - core
-    half = p // HALF
+    half = py // 2
     at_home = half == core
     own_group = z * 2 + half
-    own_channel = (p % HALF) * 2 + core
-
-    near_x = 2 * core + lax.rem(px, 2)
-    flip_x = 2 * core + 1 - lax.rem(px, 2)
-    first_x = jnp.where(at_home, flip_x, near_x)
-    last_x = jnp.where(at_home, near_x, flip_x)
+    place = lax.rem(py, 2) * 4 + px
+    own_channel = place * 2 + core
+    taps_core = p // HALF
+
+    near_y = 2 * core + lax.rem(py, 2)
+    flip_y = 2 * core + 1 - lax.rem(py, 2)
+    first_y = jnp.where(at_home, flip_y, near_y)
+    last_y = jnp.where(at_home, near_y, flip_y)
     workers = [
-        first_x * CTX_Y + ys[2], first_x * CTX_Y + ys[1], first_x * CTX_Y + ys[3], last_x * CTX_Y + ys[2],
-        last_x * CTX_Y + ys[1], last_x * CTX_Y + ys[3], first_x * CTX_Y + ys[0], last_x * CTX_Y + ys[0],
+        (xs[2], first_y), (xs[1], first_y), (xs[3], first_y), (xs[2], last_y),
+        (xs[1], last_y), (xs[3], last_y), (xs[0], first_y), (xs[0], last_y),
     ]
 
     barrier = pltpu.get_barrier_semaphore()
@@ -143,13 +143,13 @@
     def send_taps(o):
         pltpu.make_async_remote_copy(
             tap_send, tap_recv.at[p], tap_sems.at[0], tap_sems.at[1],
-            device_id=(o, z * 2 + half), device_id_type=MESH,
+            device_id=(o[0] * CTX_Y + o[1], z * 2 + taps_core), device_id_type=MESH,
         ).start()
 
     def send_signal(o, k):
         pltpu.make_async_remote_copy(
-            sig_send.at[lax.rem(o, HALF) * 2 + k], sig_recv.at[p], sig_sems.at[0], sig_sems.at[1],
-            device_id=(o, z * 2 + k), device_id_type=MESH,
+            sig_send.at[(lax.rem(o[1], 2) * 4 + o[0]) * 2 + k], sig_recv.at[p], sig_sems.at[0], sig_sems.at[1],
+            device_id=(o[0] * CTX_Y + o[1], z * 2 + k), device_id_type=MESH,
         ).start()
 
     for o in workers[:-1]:
@@ -157,25 +157,31 @@
     for o in workers[:-1]:
         send_signal(o, 0)
         send_signal(o, 1)
-    far = workers[-1]
+    keeps_taps = jnp.logical_and(at_home, taps_core == core)
+
+    @pl.when(keeps_taps)
+    def _():
+        pltpu.make_async_copy(tap_send, tap_recv.at[p], tap_sems.at[1]).start()
+
+    @pl.when(jnp.logical_not(keeps_taps))
+    def _():
+        send_taps(workers[-1])
 
     @pl.when(at_home)
     def _():
-        pltpu.make_async_copy(tap_send, tap_recv.at[p], tap_sems.at[1]).start()
-        pltpu.make_async_remote_copy(
-            sig_send.at[lax.rem(p, HALF) * 2 + 1 - core], sig_recv.at[p], sig_sems.at[0], sig_sems.at[1],
+        pltpu.make_async_remote_copy(
+            sig_send.at[place * 2 + 1 - core], sig_recv.at[p], sig_sems.at[0], sig_sems.at[1],
             device_id=(p, sibling), device_id_type=MESH,
         ).start()
         pltpu.make_async_copy(sig_send.at[own_channel], sig_recv.at[p], sig_sems.at[1]).start()
 
     @pl.when(jnp.logical_not(at_home))
     def _():
-        send_taps(far)
-        send_signal(far, 0)
-        send_signal(far, 1)
+        send_signal(workers[-1], 0)
+        send_signal(workers[-1], 1)
 
     loads[3].wait()
-    skip_send[...] = jnp.full((8, 128), skip[(p % HALF) * 2 + 1 - core], F32)
+    skip_send[...] = jnp.full((8, 128), skip[place * 2 + 1 - core], F32)
     to_sibling = pltpu.make_async_remote_copy(
         skip_send, skip_recv, skip_sems.at[0], skip_sems.at[1],
         device_id=(p, sibling), device_id_type=MESH,
@@ -260,13 +266,14 @@
         def _(o_ch=o_ch):
             send_piece(0, o_ch)
 
-    for dx, dy, dz in FAR_FIRST:
-        o_ctx = xs[dx] * CTX_Y + ys[dy]
-
-        @pl.when(o_ctx + zs[dz] != 0)
-        def _(o_ctx=o_ctx, dx=dx, dy=dy, dz=dz):
-            for dc in (0, 1) if dx or dy or dz else (1,):
-                send_piece(o_ctx, zs[dz] * 2 + cs[dc])
+    for o_z in range(4):
+        for dx, dy in FAR_FIRST:
+            o_ctx = xs[dx] * CTX_Y + ys[dy]
+            for c in range(2):
+
+                @pl.when(jnp.logical_and(o_ctx + o_z != 0, jnp.logical_or(o_ctx != p, o_z * 2 + c != g)))
+                def _(o_ctx=o_ctx, o_ch=o_z * 2 + c):
+                    send_piece(o_ctx, o_ch)
 
     pltpu.make_async_copy(y_send.at[p * CH + g], y_out.at[channel], y_sems.at[1]).start()
 
@@ -274,12 +281,18 @@
     def _():
         part = sig_send.at[pl.ds(0, 15)]
         pltpu.make_async_copy(part, part, sig_sems.at[0]).wait()
+
+    @pl.when(jnp.logical_not(at_home))
+    def _():
+        pltpu.make_async_copy(sig_send, sig_send, sig_sems.at[0]).wait()
+
+    @pl.when(keeps_taps)
+    def _():
         part = tap_recv.at[pl.ds(0, 7)]
         pltpu.make_async_copy(part, part, tap_sems.at[0]).wait()
 
-    @pl.when(jnp.logical_not(at_home))
-    def _():
-        pltpu.make_async_copy(sig_send, sig_send, sig_sems.at[0]).wait()
+    @pl.when(jnp.logical_not(keeps_taps))
+    def _():
         part = tap_recv.at[pl.ds(0, 8)]
         pltpu.make_async_copy(part, part, tap_sems.at[0]).wait()
 
@@ -293,13 +306,20 @@
     pltpu.make_async_copy(y_out, y_out, y_sems.at[1]).wait()
 
 
-def gate_kernel(y, post, out, wide):
-    wide[...] = y[...].astype(F32).reshape(wide.shape)
-    rows = out.shape[0]
-    for s in range(8):
-        at = pl.ds(s * 128, 128)
-        gate = post[:, at].astype(F32)
-        out[:, at] = (wide[pl.ds(s, rows, stride=8), :] * gate).astype(BF16)
+def gate_kernel(y, post, out, wide, made, sems):
+    rows = CTX * CH // GATE_PARTS
+    copies = []
+    for k in range(GATE_PARTS):
+        own = pl.ds(k * rows, rows)
+        wide[k] = y[own].astype(F32).reshape(rows * 8, 128)
+        for s in range(8):
+            at = pl.ds(s * 128, 128)
+            gate = post[own, at].astype(F32)
+            made[own, at] = (wide[k, pl.ds(s, rows, stride=8), :] * gate).astype(BF16)
+        copies.append(pltpu.make_async_copy(made.at[own], out.at[own], sems.at[k]))
+        copies[-1].start()
+    for copy in copies:
+        copy.wait()
 
 
 def body(pre_gate, value, post_gate, filter_taps, skip):
@@ -356,8 +376,12 @@
         gate_kernel,
         out_shape=jax.ShapeDtypeStruct((CTX * CH, PIECE), BF16),
         in_specs=[whole, whole],
-        out_specs=whole,
-        scratch_shapes=[vmem((CTX * CH * 8, 128), F32)],
+        out_specs=anyspace,
+        scratch_shapes=[
+            vmem((GATE_PARTS, CTX * CH * 8 // GATE_PARTS, 128), F32),
+            vmem((CTX * CH, PIECE), BF16),
+            dma((GATE_PARTS,)),
+        ],
         compiler_params=pltpu.CompilerParams(vmem_limit_bytes=4 * 1024 * 1024),
         name="gate",
     )(conv, gate.reshape(CTX * CH, PIECE))

time: 24.2 us -> 23.8 us (0.983)
  Pallas kernels: 24.1 us -> 23.6 us
    pallas_call x1, Pallas kernels: 23.2 us -> 22.8 us  [body(): pl.pallas_call(kernel, out_shape=[vmem((CTX * CH, 8, 128), BF16), vmem((C...]
where the time goes in v4:
time: 23.8 us; the launch traced here: 23.7 us
  Pallas kernels  23.6 us (99%)
    pallas_call x1, Pallas kernels, body(): pl.pallas_call(kernel, out_shape=[vmem((CTX * CH, 8, 128), BF16), vmem((C...  22.8 us
    pallas_call x1, Pallas kernels, body(): pl.pallas_call(gate_kernel, out_shape=jax.ShapeDtypeStruct((CTX * CH, PIE...  0.81 us

profile of v4, /device:TPU:1, one launch (start us, length us, event | category | flops | bytes accessed | tf_op | source)
XLA Modules:
  0.0 23.7 jit_solution(3211939278979923258)
XLA Ops:
  0.0 22.8 %hyena.1 = (bf16[128,8,128]{2,1,0:T(8,128)(2,1)S(1)}, bf16[8,16,1024]{2,1,0:T(8,128)(2,1)S(1)}) custom-call(bf16[16,8192]{1,0:T(8,128)(2,1)} %pre.1, bf16[16,8192]{1,0:T(8,128)(2,1)} %val.1, bf16[16,8192]{1,0:T(8,128)(2,1)} %post.1, f32[1,8192]{1,0:T(1,128)} %taps.1, f32[16]{0:T(128)} %skip_hbm.1, bf16[512,256]{1,0:T(8,128)(2,1)} %constant.10.clone.fwd_t, ...), custom_call_target="tpu_custom_call" | custom-call | tf_op jit(solution)/shard_map/hyena/pallas_call | solution.py:331
  22.8 0.8 %gate.1 = bf16[128,1024]{1,0:T(8,128)(2,1)} custom-call(bf16[128,8,128]{2,1,0:T(8,128)(2,1)S(1)} %get-tuple-element.7.y, bf16[128,1024]{1,0:T(8,128)(2,1)S(1)} %bitcast.1), custom_call_target="tpu_custom_call" | custom-call | tf_op jit(solution)/shard_map/gate/pallas_call | solution.py:375

commit v5 on v4

--- a/solution.py
+++ b/solution.py
@@ -28,6 +28,9 @@
 
 
 FAR_FIRST = sorted([(dx, dy) for dx in range(4) for dy in range(4)], key=lambda o: -(ring(o[0]) + ring(o[1])))
+
+
+COLUMN = ((2, 0), (2, 1), (1, 0), (3, 0), (1, 1), (3, 1), (0, 1))
 
 
 def pair(table, flip):
@@ -67,8 +70,8 @@
     pre, val, post, taps, skip_hbm, fwd_t, bwd_t, there_t, back_t, tw_t, y_out, post_out,
     pre_v, val_v, taps_v, fwd_v, bwd_v, there_v, back_v, tw_v,
     sig32, tap32, sig_send, tap_send, sig_recv, tap_recv, skip_send, skip_recv,
-    spec_h, y32, lin32, y_send,
-    skip, load_sems, table_sems, sig_sems, tap_sems, pass_sems, skip_sems, post_sems, y_sems,
+    spec_h, y32, lin32, y_send, y_first,
+    skip, load_sems, table_sems, sig_sems, tap_sems, pass_sems, skip_sems, post_sems, y_sems, first_sem,
 ):
     p = lax.axis_index("ctx")
     g = lax.axis_index("ch")
@@ -102,7 +105,7 @@
                 pl.semaphore_signal(
                     barrier, inc=1, device_id=(xs[dx] * CTX_Y + ys[dy], z * 2 + half), device_id_type=MESH
                 )
-    for dz, dc in ((2, 0), (2, 1), (1, 0), (3, 0), (1, 1), (3, 1), (0, 1)):
+    for dz, dc in COLUMN:
         pl.semaphore_signal(barrier, inc=1, device_id=(p, zs[dz] * 2 + cs[dc]), device_id_type=MESH)
 
     loads = [
@@ -191,13 +194,79 @@
     def post_part(o):
         return post.at[:, pl.ds(pl.multiple_of(o * PIECE, PIECE), PIECE)]
 
-    for dz, dc in ((2, 0), (2, 1), (1, 0), (3, 0), (1, 1), (3, 1), (0, 1)):
+    for dz, dc in COLUMN:
         o = zs[dz] * 2 + cs[dc]
         pltpu.make_async_remote_copy(
             post_part(o), post_out.at[g], post_sems.at[0], post_sems.at[1],
             device_id=(p, o), device_id_type=MESH,
         ).start()
     pltpu.make_async_copy(post_part(g), post_out.at[g], post_sems.at[1]).start()
+
+    def lanes(a):
+        return slice(a * 128, (a + 1) * 128)
+
+    def turn(a):
+        return tw_v[0, :, lanes(a)], tw_v[1, :, lanes(a)]
+
+    def joined(re, im):
+        return jnp.concatenate([re.astype(BF16), im.astype(BF16)], axis=1)
+
+    def spectrum(data):
+        a = jnp.dot(fwd_v[...], data, preferred_element_type=F32)
+        parts = four_point([times((a[:R, lanes(i)], a[R:, lanes(i)]), turn(i)) for i in range(4)])
+        return [
+            jnp.dot(joined(*parts[d]), there_v[d * R : (d + 1) * R, :], preferred_element_type=F32)
+            for d in range(4)
+        ]
+
+    def pieces(signal):
+        parts = []
+        for d, part in enumerate(spectrum(signal)):
+            prod = times((part[:, :128], part[:, 128:]), (spec_h[d, :, :128], spec_h[d, :, 128:]))
+            part = jnp.dot(joined(*prod), back_v[d * R : (d + 1) * R, :], preferred_element_type=F32)
+            parts.append((part[:, :128], part[:, 128:]))
+        parts = [times(part, turn(i)) for i, part in enumerate(four_point(parts))]
+        columns = jnp.concatenate(
+            [jnp.concatenate([part[i].astype(BF16) for part in parts], axis=1) for i in range(2)], axis=0
+        )
+        conv = jnp.dot(bwd_v[...], columns, preferred_element_type=F32)
+        for e in range(2):
+            for q in range(4):
+                lin32[pl.ds(e * 4 + q, 128, stride=8), :] = (
+                    conv[e * 128 : (e + 1) * 128, lanes(q)] + y32[q, pl.ds(e, 128, stride=2), :]
+                )
+        return lin32[...].reshape(CTX * CH, 8, 128).astype(BF16)
+
+    for c in tables:
+        c.wait()
+
+    @pl.when(p == 0)
+    def _():
+        gap = jnp.zeros((16, Q), BF16)
+        first = jnp.concatenate([tap_send[...], jnp.zeros((R - 16, Q), BF16)], axis=0)
+        for d, part in enumerate(spectrum(first)):
+            spec_h[d] = part
+
+        def eight_channels(r, carry):
+            rows = []
+            for i in range(8):
+                own = sig_send[r * 8 + i]
+                rows += [own, gap]
+                for q in range(4):
+                    y32[q, 32 * i : 32 * i + 16, :] = skip[r * 8 + i] * own[:, lanes(q)].astype(F32)
+                    y32[q, 32 * i + 16 : 32 * i + 32, :] = jnp.zeros((16, 128), F32)
+            y_first[r] = pieces(jnp.concatenate(rows, axis=0)).reshape(8, 16, 8, 128)
+            to = pl.ds(g * CHANNELS + r * 8, 8)
+            for dz, dc in COLUMN:
+                o = zs[dz] * 2 + cs[dc]
+                pltpu.make_async_remote_copy(
+                    y_first.at[r, :, o], y_out.at[to], first_sem, y_sems.at[1],
+                    device_id=(p, o), device_id_type=MESH,
+                ).start()
+            pltpu.make_async_copy(y_first.at[r, :, g], y_out.at[to], y_sems.at[1]).start()
+            return carry
+
+        lax.fori_loop(0, 2, eight_channels, 0)
 
     mine = tap_recv.at[pl.ds(core * HALF, HALF)]
     theirs = tap_recv.at[pl.ds((1 - core) * HALF, HALF)]
@@ -207,25 +276,6 @@
     )
     passed.start()
 
-    def lanes(a):
-        return slice(a * 128, (a + 1) * 128)
-
-    def turn(a):
-        return tw_v[0, :, lanes(a)], tw_v[1, :, lanes(a)]
-
-    def joined(re, im):
-        return jnp.concatenate([re.astype(BF16), im.astype(BF16)], axis=1)
-
-    def spectrum(data):
-        a = jnp.dot(fwd_v[...], data, preferred_element_type=F32)
-        parts = four_point([times((a[:R, lanes(i)], a[R:, lanes(i)]), turn(i)) for i in range(4)])
-        return [
-            jnp.dot(joined(*parts[d]), there_v[d * R : (d + 1) * R, :], preferred_element_type=F32)
-            for d in range(4)
-        ]
-
-    for c in tables:
-        c.wait()
     pltpu.make_async_copy(theirs, theirs, pass_sems.at[1]).wait()
     for d, part in enumerate(spectrum(tap_recv[...].reshape(R, Q))):
         spec_h[d] = part
@@ -236,22 +286,7 @@
     weight = jnp.where(at_home, skip[own_channel], skip_recv[0:1, :])
     for q in range(4):
         y32[q] = weight * signal[:, lanes(q)].astype(F32)
-    parts = []
-    for d, part in enumerate(spectrum(signal)):
-        prod = times((part[:, :128], part[:, 128:]), (spec_h[d, :, :128], spec_h[d, :, 128:]))
-        part = jnp.dot(joined(*prod), back_v[d * R : (d + 1) * R, :], preferred_element_type=F32)
-        parts.append((part[:, :128], part[:, 128:]))
-    parts = [times(part, turn(i)) for i, part in enumerate(four_point(parts))]
-    columns = jnp.concatenate(
-        [jnp.concatenate([part[i].astype(BF16) for part in parts], axis=1) for i in range(2)], axis=0
-    )
-    conv = jnp.dot(bwd_v[...], columns, preferred_element_type=F32)
-    for e in range(2):
-        for q in range(4):
-            lin32[pl.ds(e * 4 + q, 128, stride=8), :] = (
-                conv[e * 128 : (e + 1) * 128, lanes(q)] + y32[q, pl.ds(e, 128, stride=2), :]
-            )
-    y_send[...] = lin32[...].reshape(CTX * CH, 8, 128).astype(BF16)
+    y_send[...] = pieces(signal)
 
     channel = own_group * CHANNELS + own_channel
     def send_piece(o_ctx, o_ch):
@@ -260,22 +295,25 @@
             device_id=(o_ctx, o_ch), device_id_type=MESH,
         ).start()
 
-    for o_ch in (1, 0):
-
-        @pl.when(jnp.logical_or(p != 0, g != o_ch))
-        def _(o_ch=o_ch):
-            send_piece(0, o_ch)
-
     for o_z in range(4):
         for dx, dy in FAR_FIRST:
             o_ctx = xs[dx] * CTX_Y + ys[dy]
-            for c in range(2):
-
-                @pl.when(jnp.logical_and(o_ctx + o_z != 0, jnp.logical_or(o_ctx != p, o_z * 2 + c != g)))
-                def _(o_ctx=o_ctx, o_ch=o_z * 2 + c):
-                    send_piece(o_ctx, o_ch)
-
-    pltpu.make_async_copy(y_send.at[p * CH + g], y_out.at[channel], y_sems.at[1]).start()
+
+            @pl.when(o_ctx != 0)
+            def _(o_ctx=o_ctx, o_z=o_z, same=not (dx or dy)):
+                for c in range(2):
+                    if same:
+
+                        @pl.when(g != o_z * 2 + c)
+                        def _(c=c):
+                            send_piece(o_ctx, o_z * 2 + c)
+
+                    else:
+                        send_piece(o_ctx, o_z * 2 + c)
+
+    @pl.when(p != 0)
+    def _():
+        pltpu.make_async_copy(y_send.at[p * CH + g], y_out.at[channel], y_sems.at[1]).start()
 
     @pl.when(at_home)
     def _():
@@ -301,8 +339,19 @@
     part = post_out.at[pl.ds(0, CH - 1)]
     pltpu.make_async_copy(part, part, post_sems.at[0]).wait()
     pltpu.make_async_copy(post_out, post_out, post_sems.at[1]).wait()
-    part = y_send.at[pl.ds(0, CTX * CH - 1)]
-    pltpu.make_async_copy(part, part, y_sems.at[0]).wait()
+
+    @pl.when(p == 0)
+    def _():
+        part = y_send.at[pl.ds(0, (CTX - 1) * CH)]
+        pltpu.make_async_copy(part, part, y_sems.at[0]).wait()
+        part = y_send.at[pl.ds(0, 2 * 8 * (CH - 1))]
+        pltpu.make_async_copy(part, part, first_sem).wait()
+
+    @pl.when(p != 0)
+    def _():
+        part = y_send.at[pl.ds(0, (CTX - 1) * CH - 1)]
+        pltpu.make_async_copy(part, part, y_sems.at[0]).wait()
+
     pltpu.make_async_copy(y_out, y_out, y_sems.at[1]).wait()
 
 
@@ -357,6 +406,7 @@
             vmem((4, R, 128), F32),
             vmem((CTX * CH * 8, 128), F32),
             vmem((CTX * CH, 8, 128), BF16),
+            vmem((2, 8, 16, 8, 128), BF16),
             pltpu.SMEM((16,), F32),
             dma((4,)),
             dma((5,)),
@@ -366,6 +416,7 @@
             dma((2,)),
             dma((2,)),
             dma((2,)),
+            dma,
         ],
         compiler_params=pltpu.CompilerParams(
             collective_id=0, has_side_effects=True, vmem_limit_bytes=56 * 1024 * 1024

time: 23.8 us -> 22.3 us (0.937)
  the two profiles are of different devices: /device:TPU:1 before, /device:TPU:3 now
where the time goes in v5:
time: 22.3 us; the launch traced here: 22.2 us
  Pallas kernels  22.2 us (100%)
    pallas_call x1, Pallas kernels, body(): pl.pallas_call(kernel, out_shape=[vmem((CTX * CH, 8, 128), BF16), vmem((C...  21.4 us
    pallas_call x1, Pallas kernels, body(): pl.pallas_call(gate_kernel, out_shape=jax.ShapeDtypeStruct((CTX * CH, PIE...  0.81 us

profile of v5, /device:TPU:3, one launch (start us, length us, event | category | flops | bytes accessed | tf_op | source)
XLA Modules:
  0.0 22.2 jit_solution(8365201328717436974)
XLA Ops:
  0.0 21.4 %hyena.1 = (bf16[128,8,128]{2,1,0:T(8,128)(2,1)S(1)}, bf16[8,16,1024]{2,1,0:T(8,128)(2,1)S(1)}) custom-call(bf16[16,8192]{1,0:T(8,128)(2,1)} %pre.1, bf16[16,8192]{1,0:T(8,128)(2,1)} %val.1, bf16[16,8192]{1,0:T(8,128)(2,1)} %post.1, f32[1,8192]{1,0:T(1,128)} %taps.1, f32[16]{0:T(128)} %skip_hbm.1, bf16[512,256]{1,0:T(8,128)(2,1)} %constant.10.clone.fwd_t, ...), custom_call_target="tpu_custom_call" | custom-call | tf_op jit(solution)/shard_map/hyena/pallas_call | solution.py:380
  21.4 0.8 %gate.1 = bf16[128,1024]{1,0:T(8,128)(2,1)} custom-call(bf16[128,8,128]{2,1,0:T(8,128)(2,1)S(1)} %get-tuple-element.7.y, bf16[128,1024]{1,0:T(8,128)(2,1)S(1)} %bitcast.1), custom_call_target="tpu_custom_call" | custom-call | tf_op jit(solution)/shard_map/gate/pallas_call | solution.py:426

commit v6 on v5

--- a/solution.py
+++ b/solution.py
@@ -157,9 +157,9 @@
 
     for o in workers[:-1]:
         send_taps(o)
-    for o in workers[:-1]:
-        send_signal(o, 0)
-        send_signal(o, 1)
+    for k in range(2):
+        for o in workers[:-1]:
+            send_signal(o, k)
     keeps_taps = jnp.logical_and(at_home, taps_core == core)
 
     @pl.when(keeps_taps)

time: 22.3 us -> 21.9 us (0.982)
  Pallas kernels: 22.2 us -> 21.8 us
    pallas_call x1, Pallas kernels: 21.4 us -> 21 us  [body(): pl.pallas_call(kernel, out_shape=[vmem((CTX * CH, 8, 128), BF16), vmem((C...]
where the time goes in v6:
time: 21.9 us; the launch traced here: 21.8 us
  Pallas kernels  21.8 us (100%)
    pallas_call x1, Pallas kernels, body(): pl.pallas_call(kernel, out_shape=[vmem((CTX * CH, 8, 128), BF16), vmem((C...  21 us
    pallas_call x1, Pallas kernels, body(): pl.pallas_call(gate_kernel, out_shape=jax.ShapeDtypeStruct((CTX * CH, PIE...  0.81 us

profile of v6, /device:TPU:3, one launch (start us, length us, event | category | flops | bytes accessed | tf_op | source)
XLA Modules:
  0.0 21.8 jit_solution(17233012001310163266)
XLA Ops:
  0.0 21.0 %hyena.1 = (bf16[128,8,128]{2,1,0:T(8,128)(2,1)S(1)}, bf16[8,16,1024]{2,1,0:T(8,128)(2,1)S(1)}) custom-call(bf16[16,8192]{1,0:T(8,128)(2,1)} %pre.1, bf16[16,8192]{1,0:T(8,128)(2,1)} %val.1, bf16[16,8192]{1,0:T(8,128)(2,1)} %post.1, f32[1,8192]{1,0:T(1,128)} %taps.1, f32[16]{0:T(128)} %skip_hbm.1, bf16[512,256]{1,0:T(8,128)(2,1)} %constant.10.clone.fwd_t, ...), custom_call_target="tpu_custom_call" | custom-call | tf_op jit(solution)/shard_map/hyena/pallas_call | solution.py:380
  21.0 0.8 %gate.1 = bf16[128,1024]{1,0:T(8,128)(2,1)} custom-call(bf16[128,8,128]{2,1,0:T(8,128)(2,1)S(1)} %get-tuple-element.7.y, bf16[128,1024]{1,0:T(8,128)(2,1)S(1)} %bitcast.1), custom_call_target="tpu_custom_call" | custom-call | tf_op jit(solution)/shard_map/gate/pallas_call | solution.py:426

commit v7 on v6

--- a/solution.py
+++ b/solution.py
@@ -44,7 +44,8 @@
     part = np.arange(128)
     first = 2 * np.pi * ((np.outer(2 * rows + 1, rows)) % 1024) / 1024.0
     forward = np.concatenate([np.cos(first), -np.sin(first)], axis=0)
-    order = np.concatenate([rows[0::2], rows[1::2]])
+    pairs = rows.reshape(CTX, 2, 4, 2)
+    order = pairs.transpose(1, 3, 0, 2).reshape(-1)
     backward = np.concatenate([np.cos(first).T, np.sin(first).T], axis=1)[order] * (2.0**-17)
     turn = 2 * np.pi * np.outer(2 * rows + 1, cols) / 2.0**19
     twiddle = np.stack([np.cos(turn), -np.sin(turn)])
@@ -70,7 +71,7 @@
     pre, val, post, taps, skip_hbm, fwd_t, bwd_t, there_t, back_t, tw_t, y_out, post_out,
     pre_v, val_v, taps_v, fwd_v, bwd_v, there_v, back_v, tw_v,
     sig32, tap32, sig_send, tap_send, sig_recv, tap_recv, skip_send, skip_recv,
-    spec_h, y32, lin32, y_send, y_first,
+    spec_h, y32, direct, lin32, y_send, y_first,
     skip, load_sems, table_sems, sig_sems, tap_sems, pass_sems, skip_sems, post_sems, y_sems, first_sem,
 ):
     p = lax.axis_index("ctx")
@@ -219,23 +220,27 @@
             for d in range(4)
         ]
 
-    def pieces(signal):
+    def answer(signal):
+        for e in range(2):
+            for q in range(4):
+                direct[pl.ds(e * 4 + q, 128, stride=8), :] = y32[q, pl.ds(e, 128, stride=2), :]
         parts = []
         for d, part in enumerate(spectrum(signal)):
             prod = times((part[:, :128], part[:, 128:]), (spec_h[d, :, :128], spec_h[d, :, 128:]))
             part = jnp.dot(joined(*prod), back_v[d * R : (d + 1) * R, :], preferred_element_type=F32)
             parts.append((part[:, :128], part[:, 128:]))
         parts = [times(part, turn(i)) for i, part in enumerate(four_point(parts))]
-        columns = jnp.concatenate(
+        return jnp.concatenate(
             [jnp.concatenate([part[i].astype(BF16) for part in parts], axis=1) for i in range(2)], axis=0
         )
-        conv = jnp.dot(bwd_v[...], columns, preferred_element_type=F32)
+
+    def pieces(columns, h):
+        conv = jnp.dot(bwd_v[h * 128 : (h + 1) * 128], columns, preferred_element_type=F32)
         for e in range(2):
             for q in range(4):
-                lin32[pl.ds(e * 4 + q, 128, stride=8), :] = (
-                    conv[e * 128 : (e + 1) * 128, lanes(q)] + y32[q, pl.ds(e, 128, stride=2), :]
-                )
-        return lin32[...].reshape(CTX * CH, 8, 128).astype(BF16)
+                lin32[h, pl.ds(e * 4 + q, 64, stride=8), :] = conv[e * 64 : (e + 1) * 64, lanes(q)]
+        total = lin32[h].reshape(CTX, 32, 128) + direct[...].reshape(CTX, 2, 32, 128)[:, h]
+        return total.reshape(CTX, 4, 8, 128).astype(BF16)
 
     for c in tables:
         c.wait()
@@ -255,7 +260,11 @@
                 for q in range(4):
                     y32[q, 32 * i : 32 * i + 16, :] = skip[r * 8 + i] * own[:, lanes(q)].astype(F32)
                     y32[q, 32 * i + 16 : 32 * i + 32, :] = jnp.zeros((16, 128), F32)
-            y_first[r] = pieces(jnp.concatenate(rows, axis=0)).reshape(8, 16, 8, 128)
+            columns = answer(jnp.concatenate(rows, axis=0))
+            for h in range(2):
+                part = pieces(columns, h).reshape(8, 2, 4, 8, 128)
+                for k in range(2):
+                    y_first[r, :, k * 8 + 4 * h : k * 8 + 4 * h + 4] = part[:, k]
             to = pl.ds(g * CHANNELS + r * 8, 8)
             for dz, dc in COLUMN:
                 o = zs[dz] * 2 + cs[dc]
@@ -286,16 +295,18 @@
     weight = jnp.where(at_home, skip[own_channel], skip_recv[0:1, :])
     for q in range(4):
         y32[q] = weight * signal[:, lanes(q)].astype(F32)
-    y_send[...] = pieces(signal)
+    columns = answer(signal)
 
     channel = own_group * CHANNELS + own_channel
     def send_piece(o_ctx, o_ch):
         pltpu.make_async_remote_copy(
-            y_send.at[o_ctx * CH + o_ch], y_out.at[channel], y_sems.at[0], y_sems.at[1],
+            y_send.at[o_ctx, o_ch], y_out.at[channel], y_sems.at[0], y_sems.at[1],
             device_id=(o_ctx, o_ch), device_id_type=MESH,
         ).start()
 
     for o_z in range(4):
+        if o_z % 2 == 0:
+            y_send[:, o_z * 2 : o_z * 2 + 4] = pieces(columns, o_z // 2)
         for dx, dy in FAR_FIRST:
             o_ctx = xs[dx] * CTX_Y + ys[dy]
 
@@ -313,7 +324,7 @@
 
     @pl.when(p != 0)
     def _():
-        pltpu.make_async_copy(y_send.at[p * CH + g], y_out.at[channel], y_sems.at[1]).start()
+        pltpu.make_async_copy(y_send.at[p, g], y_out.at[channel], y_sems.at[1]).start()
 
     @pl.when(at_home)
     def _():
@@ -342,14 +353,14 @@
 
     @pl.when(p == 0)
     def _():
-        part = y_send.at[pl.ds(0, (CTX - 1) * CH)]
+        part = y_out.at[pl.ds(0, (CTX - 1) * CH)]
         pltpu.make_async_copy(part, part, y_sems.at[0]).wait()
-        part = y_send.at[pl.ds(0, 2 * 8 * (CH - 1))]
+        part = y_out.at[pl.ds(0, 2 * 8 * (CH - 1))]
         pltpu.make_async_copy(part, part, first_sem).wait()
 
     @pl.when(p != 0)
     def _():
-        part = y_send.at[pl.ds(0, (CTX - 1) * CH - 1)]
+        part = y_out.at[pl.ds(0, (CTX - 1) * CH - 1)]
         pltpu.make_async_copy(part, part, y_sems.at[0]).wait()
 
     pltpu.make_async_copy(y_out, y_out, y_sems.at[1]).wait()
@@ -405,7 +416,8 @@
             vmem((4, R, 2 * 128), F32),
             vmem((4, R, 128), F32),
             vmem((CTX * CH * 8, 128), F32),
-            vmem((CTX * CH, 8, 128), BF16),
+            vmem((2, CTX * CH * 4, 128), F32),
+            vmem((CTX, CH, 8, 128), BF16),
             vmem((2, 8, 16, 8, 128), BF16),
             pltpu.SMEM((16,), F32),
             dma((4,)),

time: 21.9 us -> 21.9 us (level)
  no operation moved by 1% of the time
where the time goes in v7:
time: 21.9 us; the launch traced here: 21.8 us
  Pallas kernels  21.8 us (100%)
    pallas_call x1, Pallas kernels, body(): pl.pallas_call(kernel, out_shape=[vmem((CTX * CH, 8, 128), BF16), vmem((C...  21 us
    pallas_call x1, Pallas kernels, body(): pl.pallas_call(gate_kernel, out_shape=jax.ShapeDtypeStruct((CTX * CH, PIE...  0.81 us

profile of v7, /device:TPU:3, one launch (start us, length us, event | category | flops | bytes accessed | tf_op | source)
XLA Modules:
  0.0 21.8 jit_solution(13733473344045449291)
XLA Ops:
  0.0 21.0 %hyena.1 = (bf16[128,8,128]{2,1,0:T(8,128)(2,1)S(1)}, bf16[8,16,1024]{2,1,0:T(8,128)(2,1)S(1)}) custom-call(bf16[16,8192]{1,0:T(8,128)(2,1)} %pre.1, bf16[16,8192]{1,0:T(8,128)(2,1)} %val.1, bf16[16,8192]{1,0:T(8,128)(2,1)} %post.1, f32[1,8192]{1,0:T(1,128)} %taps.1, f32[16]{0:T(128)} %skip_hbm.1, bf16[512,256]{1,0:T(8,128)(2,1)} %constant.10.clone.fwd_t, ...), custom_call_target="tpu_custom_call" | custom-call | tf_op jit(solution)/shard_map/hyena/pallas_call | solution.py:391
  21.0 0.8 %gate.1 = bf16[128,1024]{1,0:T(8,128)(2,1)} custom-call(bf16[128,8,128]{2,1,0:T(8,128)(2,1)S(1)} %get-tuple-element.7.y, bf16[128,1024]{1,0:T(8,128)(2,1)S(1)} %bitcast.1), custom_call_target="tpu_custom_call" | custom-call | tf_op jit(solution)/shard_map/gate/pallas_call | solution.py:438

commit v8 on v7

--- a/solution.py
+++ b/solution.py
@@ -44,7 +44,7 @@
     part = np.arange(128)
     first = 2 * np.pi * ((np.outer(2 * rows + 1, rows)) % 1024) / 1024.0
     forward = np.concatenate([np.cos(first), -np.sin(first)], axis=0)
-    pairs = rows.reshape(CTX, 2, 4, 2)
+    pairs = rows.reshape(CTX, 4, 2, 2)
     order = pairs.transpose(1, 3, 0, 2).reshape(-1)
     backward = np.concatenate([np.cos(first).T, np.sin(first).T], axis=1)[order] * (2.0**-17)
     turn = 2 * np.pi * np.outer(2 * rows + 1, cols) / 2.0**19
@@ -235,12 +235,12 @@
         )
 
     def pieces(columns, h):
-        conv = jnp.dot(bwd_v[h * 128 : (h + 1) * 128], columns, preferred_element_type=F32)
+        conv = jnp.dot(bwd_v[h * 64 : (h + 1) * 64], columns, preferred_element_type=F32)
         for e in range(2):
             for q in range(4):
-                lin32[h, pl.ds(e * 4 + q, 64, stride=8), :] = conv[e * 64 : (e + 1) * 64, lanes(q)]
-        total = lin32[h].reshape(CTX, 32, 128) + direct[...].reshape(CTX, 2, 32, 128)[:, h]
-        return total.reshape(CTX, 4, 8, 128).astype(BF16)
+                lin32[h, pl.ds(e * 4 + q, 32, stride=8), :] = conv[e * 32 : (e + 1) * 32, lanes(q)]
+        total = lin32[h].reshape(CTX, 16, 128) + direct[...].reshape(CTX, 4, 16, 128)[:, h]
+        return total.reshape(CTX, 2, 8, 128).astype(BF16)
 
     for c in tables:
         c.wait()
@@ -261,10 +261,10 @@
                     y32[q, 32 * i : 32 * i + 16, :] = skip[r * 8 + i] * own[:, lanes(q)].astype(F32)
                     y32[q, 32 * i + 16 : 32 * i + 32, :] = jnp.zeros((16, 128), F32)
             columns = answer(jnp.concatenate(rows, axis=0))
-            for h in range(2):
-                part = pieces(columns, h).reshape(8, 2, 4, 8, 128)
+            for h in range(4):
+                part = pieces(columns, h).reshape(8, 2, 2, 8, 128)
                 for k in range(2):
-                    y_first[r, :, k * 8 + 4 * h : k * 8 + 4 * h + 4] = part[:, k]
+                    y_first[r, :, k * 8 + 2 * h : k * 8 + 2 * h + 2] = part[:, k]
             to = pl.ds(g * CHANNELS + r * 8, 8)
             for dz, dc in COLUMN:
                 o = zs[dz] * 2 + cs[dc]
@@ -305,22 +305,20 @@
         ).start()
 
     for o_z in range(4):
-        if o_z % 2 == 0:
-            y_send[:, o_z * 2 : o_z * 2 + 4] = pieces(columns, o_z // 2)
-        for dx, dy in FAR_FIRST:
+        y_send[:, o_z * 2 : o_z * 2 + 2] = pieces(columns, o_z)
+        for c, (dx, dy) in [(c, o) for c in range(2) for o in FAR_FIRST]:
             o_ctx = xs[dx] * CTX_Y + ys[dy]
 
             @pl.when(o_ctx != 0)
-            def _(o_ctx=o_ctx, o_z=o_z, same=not (dx or dy)):
-                for c in range(2):
-                    if same:
-
-                        @pl.when(g != o_z * 2 + c)
-                        def _(c=c):
-                            send_piece(o_ctx, o_z * 2 + c)
-
-                    else:
+            def _(o_ctx=o_ctx, o_z=o_z, c=c, same=not (dx or dy)):
+                if same:
+
+                    @pl.when(g != o_z * 2 + c)
+                    def _():
                         send_piece(o_ctx, o_z * 2 + c)
+
+                else:
+                    send_piece(o_ctx, o_z * 2 + c)
 
     @pl.when(p != 0)
     def _():
@@ -416,7 +414,7 @@
             vmem((4, R, 2 * 128), F32),
             vmem((4, R, 128), F32),
             vmem((CTX * CH * 8, 128), F32),
-            vmem((2, CTX * CH * 4, 128), F32),
+            vmem((4, CTX * CH * 2, 128), F32),
             vmem((CTX, CH, 8, 128), BF16),
             vmem((2, 8, 16, 8, 128), BF16),
             pltpu.SMEM((16,), F32),

time: 21.9 us -> 21.8 us (level)
  no operation moved by 1% of the time
where the time goes in v8:
time: 21.8 us; the launch traced here: 21.7 us
  Pallas kernels  21.7 us (100%)
    pallas_call x1, Pallas kernels, body(): pl.pallas_call(kernel, out_shape=[vmem((CTX * CH, 8, 128), BF16), vmem((C...  20.9 us
    pallas_call x1, Pallas kernels, body(): pl.pallas_call(gate_kernel, out_shape=jax.ShapeDtypeStruct((CTX * CH, PIE...  0.81 us

profile of v8, /device:TPU:3, one launch (start us, length us, event | category | flops | bytes accessed | tf_op | source)
XLA Modules:
  0.0 21.7 jit_solution(655723217523056676)
XLA Ops:
  0.0 20.9 %hyena.1 = (bf16[128,8,128]{2,1,0:T(8,128)(2,1)S(1)}, bf16[8,16,1024]{2,1,0:T(8,128)(2,1)S(1)}) custom-call(bf16[16,8192]{1,0:T(8,128)(2,1)} %pre.1, bf16[16,8192]{1,0:T(8,128)(2,1)} %val.1, bf16[16,8192]{1,0:T(8,128)(2,1)} %post.1, f32[1,8192]{1,0:T(1,128)} %taps.1, f32[16]{0:T(128)} %skip_hbm.1, bf16[512,256]{1,0:T(8,128)(2,1)} %constant.10.clone.fwd_t, ...), custom_call_target="tpu_custom_call" | custom-call | tf_op jit(solution)/shard_map/hyena/pallas_call | solution.py:389
  20.9 0.8 %gate.1 = bf16[128,1024]{1,0:T(8,128)(2,1)} custom-call(bf16[128,8,128]{2,1,0:T(8,128)(2,1)S(1)} %get-tuple-element.7.y, bf16[128,1024]{1,0:T(8,128)(2,1)S(1)} %bitcast.1), custom_call_target="tpu_custom_call" | custom-call | tf_op jit(solution)/shard_map/gate/pallas_call | solution.py:436

commit v9 on v7

--- a/solution.py
+++ b/solution.py
@@ -312,7 +312,7 @@
 
             @pl.when(o_ctx != 0)
             def _(o_ctx=o_ctx, o_z=o_z, same=not (dx or dy)):
-                for c in range(2):
+                for c in (1, 0):
                     if same:
 
                         @pl.when(g != o_z * 2 + c)

time: 21.9 us -> 21.9 us (level)
  the two profiles are of different devices: /device:TPU:3 before, /device:TPU:2 now
where the time goes in v9:
time: 21.9 us; the launch traced here: 21.8 us
  Pallas kernels  21.8 us (100%)
    pallas_call x1, Pallas kernels, body(): pl.pallas_call(kernel, out_shape=[vmem((CTX * CH, 8, 128), BF16), vmem((C...  21 us
    pallas_call x1, Pallas kernels, body(): pl.pallas_call(gate_kernel, out_shape=jax.ShapeDtypeStruct((CTX * CH, PIE...  0.81 us

profile of v9, /device:TPU:2, one launch (start us, length us, event | category | flops | bytes accessed | tf_op | source)
XLA Modules:
  0.0 21.8 jit_solution(14473301005118126552)
XLA Ops:
  0.0 21.0 %hyena.1 = (bf16[128,8,128]{2,1,0:T(8,128)(2,1)S(1)}, bf16[8,16,1024]{2,1,0:T(8,128)(2,1)S(1)}) custom-call(bf16[16,8192]{1,0:T(8,128)(2,1)} %pre.1, bf16[16,8192]{1,0:T(8,128)(2,1)} %val.1, bf16[16,8192]{1,0:T(8,128)(2,1)} %post.1, f32[1,8192]{1,0:T(1,128)} %taps.1, f32[16]{0:T(128)} %skip_hbm.1, bf16[512,256]{1,0:T(8,128)(2,1)} %constant.10.clone.fwd_t, ...), custom_call_target="tpu_custom_call" | custom-call | tf_op jit(solution)/shard_map/hyena/pallas_call | solution.py:391
  21.0 0.8 %gate.1 = bf16[128,1024]{1,0:T(8,128)(2,1)} custom-call(bf16[128,8,128]{2,1,0:T(8,128)(2,1)S(1)} %get-tuple-element.7.y, bf16[128,1024]{1,0:T(8,128)(2,1)S(1)} %bitcast.1), custom_call_target="tpu_custom_call" | custom-call | tf_op jit(solution)/shard_map/gate/pallas_call | solution.py:438
